TPU v7x, 32 devices: a whole 2x2x4 slice. The times are simulated.
32 devices in a mesh: grp: 2 (over x), ex: 16 (over z, y, core).
Axes of the slice: x: 2, y: 2, z: 4, core: 2. Of those that a mesh axis runs over, the one named last changes fastest.
Arguments:
- values_store: bfloat16 [15360, 3, 2048], P('ex'), may hold values from -7.5 to 7.5, as said below
- scale_exps: int32 [15360, 3, 16], P('ex'), may hold values from -2 to 2
- test_grads: bfloat16 [3, 2048, 512], P(None, 'ex', 'grp'), parts along dimension 2, may hold values from -64 to 64
- lr_weights: float32 [3], replicated, may hold values from 0.3 to 3
- example_weights: float32 [15360], P('ex'), may hold values from 1 to 31
Outputs:
- influence: float32 [15360, 512], P('ex', 'grp'), parts along dimension 1
There are 2 independent parts, one for each index of `grp`. A program takes and returns all parts, laid end to end along the dimension named above; an argument that names none is the same for every part. Nothing has to cross between parts.
Inputs may be any that keep to these rules, and one draw needn't show every extreme that they name: `values_store`: each value is s (8 + m) / 8 times 2 ** e with s = 1 or -1, m an integer 0 to 7 and e an integer -3 to 2.
All inputs are finite; a program needn't handle non-finite values.
Results may differ from a plain program's by a relative error of at most 0.0003.
Values may be sent and summed in bfloat16 or wider, within the bound.
A program may use at most 128 MiB of HBM per device.

v0:
```python
import jax
import jax.numpy as jnp
from jax import lax
from jax.sharding import PartitionSpec as P

EPSILON = 1e-06


def dequantize(values_store, scale_exps):
    factor = jnp.exp2(scale_exps.astype(jnp.float32)).astype(jnp.bfloat16)
    shaped = values_store.reshape(values_store.shape[:-1] + (scale_exps.shape[-1], -1))
    return (shaped * factor[..., None]).reshape(values_store.shape)


def checkpoint_sum(train_vals, test_block, lr_weights):
    partial_value = lr_weights[0] * jnp.dot(
        train_vals[:, 0, :], test_block[0], preferred_element_type=jnp.float32
    )
    for ckpt_index in range(1, train_vals.shape[1]):
        partial_value = partial_value + lr_weights[ckpt_index] * jnp.dot(
            train_vals[:, ckpt_index, :], test_block[ckpt_index], preferred_element_type=jnp.float32
        )
    return partial_value


def on_device(values_store, scale_exps, test_grads, lr_weights, example_weights):
    train_vals = dequantize(values_store, scale_exps)
    gathered = lax.all_gather(test_grads, "ex", axis=1, tiled=True)
    partial_value = checkpoint_sum(train_vals, gathered, lr_weights)
    weighted = example_weights[:, None] * partial_value
    square_sums = lax.psum(jnp.sum(weighted * weighted, axis=0), "ex")
    examples_all = weighted.shape[0] * lax.axis_size("ex")
    return weighted / jnp.sqrt(square_sums / examples_all + EPSILON)


def solution(mesh):
    return jax.shard_map(
        on_device,
        mesh=mesh,
        in_specs=(P("ex", None, None), P("ex", None, None), P(None, "ex", "grp"), P(), P("ex")),
        out_specs=P("ex", "grp"),
        check_vma=False,
    )
```

profile of v0, /device:TPU:0, one launch (start us, length us, event | category | flops | bytes accessed | tf_op | source)
XLA Modules:
  0.0 108.9 jit_solution(5403036772866053238)
XLA Ops:
  6.5 0.0 all-gather.2.cloned.1.call-start
  6.5 0.7 all-gather.2.cloned.1.call-update
  7.3 1.0 exponential_convert_fusion
  8.2 0.4 copy.6
  8.6 8.0 %mul.42 = bf16[960,3,16,128]{3,2,0,1:T(8,128)(2,1)} broadcast(bf16[960,3,16]{2,0,1:T(8,128)(2,1)S(1)} %copy.6), dimensions={0,1,2} | broadcast | bytes 11888640 | tf_op jit(solution)/shard_map/mul | solution.py:12
  16.6 18.6 %mul.43 = bf16[960,3,2048]{2,0,1:T(8,128)(2,1)} reshape(bf16[960,3,16,128]{3,2,0,1:T(8,128)(2,1)} %mul.42) | data formatting | bytes 23592960 | tf_op jit(solution)/shard_map/mul | solution.py:12
  35.1 0.0 copy-start.1
  35.1 14.5 %mul.44 = bf16[960,3,2048]{2,0,1:T(8,128)(2,1)} multiply(bf16[960,3,2048]{2,0,1:T(8,128)(2,1)} %param.5, bf16[960,3,2048]{2,0,1:T(8,128)(2,1)} %mul.43) | non-fusion elementwise | flops 5898240 | bytes 35389440 | tf_op jit(solution)/shard_map/mul | solution.py:12
  49.7 0.0 copy-done.1
  49.7 0.6 fusion.9
  50.3 7.2 %all-gather.2.cloned.1.call-done = bf16[3,2048,256]{2,1,0:T(8,128)(2,1)} async-done(((bf16[3,128,256]{2,1,0:T(8,128)(2,1)}), bf16[3,2048,256]{2,1,0:T(8,128)(2,1)}) %all-gather.2.cloned.1.call-update) | async-done | bytes 3145744 | tf_op jit(solution)/shard_map/all_gather | solution.py:28
  57.5 0.0 copy-start
  57.5 4.5 %fusion.7 = f32[960,256]{1,0:T(8,128)S(1)} fusion(bf16[960,3,2048]{2,0,1:T(8,128)(2,1)} %mul.44, bf16[3,2048,256]{2,1,0:T(8,128)(2,1)} %all-gather.2.cloned.1.call-done, f32[]{:T(128)} %bitcast.3), kind=kOutput, calls=%fused_computation.10 | convolution fusion | flops 1006878720 | bytes 5964288 | tf_op jit(solution)/shard_map/dot_general | solution.py:20
  62.0 1.4 %copy-done = bf16[960,3,2048]{2,0,1:T(8,128)(2,1)S(1)} copy-done((bf16[960,3,2048]{2,0,1:T(8,128)(2,1)S(1)}, bf16[960,3,2048]{2,0,1:T(8,128)(2,1)}, u32[]{:S(2)}) %copy-start) | copy-done | bytes 11796504
  63.3 0.0 copy-start.2
  63.3 3.1 %fusion.8 = f32[960,256]{1,0:T(8,128)S(1)} fusion(bf16[960,3,2048]{2,0,1:T(8,128)(2,1)S(1)} %copy-done, bf16[3,2048,256]{2,1,0:T(8,128)(2,1)} %all-gather.2.cloned.1.call-done, f32[]{:T(128)} %bitcast.6), kind=kOutput, calls=%fused_computation.11 | convolution fusion | flops 1006878720 | bytes 5964288 | tf_op jit(solution)/shard_map/dot_general | solution.py:20
  66.4 0.0 copy-done.2
  66.4 3.1 %multiply_reduce_fusion = (f32[256]{0:T(256)S(1)}, f32[960,256]{1,0:T(8,128)S(1)}) fusion(f32[960,256]{1,0:T(8,128)S(1)} %fusion.8, f32[960,256]{1,0:T(8,128)S(1)} %fusion.7, bf16[3,2048,256]{2,1,0:T(8,128)(2,1)} %all-gather.2.cloned.1.call-done, bf16[960,3,2048]{2,0,1:T(8,128)(2,1)S(1)} %copy-done, f32[]{:T(128)} %bitcast, f32[960]{0:T(1024)S(1)} %copy-done.2), kind=kOutput, calls=%fused_computation.15 | convolution fusion | flops 1008107264 | bytes 7935488 | tf_op jit(solution)/shard_map/dot_general | solution.py:16
  69.5 31.5 %psum.7 = f32[256]{0:T(256)S(1)} all-reduce(f32[256]{0:T(256)S(1)} %get-tuple-element.8), channel_id=1, replica_groups=mesh['grp'=2,'ex'=16] {'ex'}, use_global_device_ids=true, to_apply=%region_1.0 | all-reduce | flops 256 | bytes 2048 | tf_op jit(solution)/shard_map/psum | solution.py:31
  101.0 1.0 broadcast_divide_fusion
  (1 shorter events, 0.0 us)
Async XLA Ops:
  6.5 51.0 %all-gather.2.cloned.1.call-start = ((), (), s32[]{:S(2)}) async-start(), calls=%async_computation | async-start | bytes 3342336 | tf_op jit(solution)/shard_map/all_gather | solution.py:28
  35.1 14.6 %copy-start.1 = (f32[3]{0:T(128)S(1)}, f32[3]{0:T(128)}, u32[]{:S(2)}) copy-start(f32[3]{0:T(128)} %param.8) | copy-start | bytes 40
  57.5 5.9 %copy-start = (bf16[960,3,2048]{2,0,1:T(8,128)(2,1)S(1)}, bf16[960,3,2048]{2,0,1:T(8,128)(2,1)}, u32[]{:S(2)}) copy-start(bf16[960,3,2048]{2,0,1:T(8,128)(2,1)} %mul.44) | copy-start | bytes 35389444
  63.3 3.1 %copy-start.2 = (f32[960]{0:T(1024)S(1)}, f32[960]{0:T(1024)}, u32[]{:S(2)}) copy-start(f32[960]{0:T(1024)} %param.9) | copy-start | bytes 11524
Sparse Core Ops, SparseCore 0:
  9.5 47.9 all-gather.1
where the time goes:
time: 110 us; the launch traced here: 109 us
  blocking collectives  31.5 us (29%)
  local copies, waits for them, and re-layouts  29 us (26%)
  other arithmetic  16.5 us (15%)
  between operations  13.4 us (12%)
  matrix products  10.6 us (10%)
  waiting for transfers between devices  7.86 us (7%)
    psum x1, blocking collectives, on_device(): square_sums = lax.psum(jnp.sum(weighted * weighted, axis=0), 'ex')  31.5 us
    mul x2, local copies, waits for them, and re-layouts, dequantize(): return (shaped * factor[..., None]).reshape(values_store.shape)  26.6 us
    mul x1, other arithmetic, dequantize(): return (shaped * factor[..., None]).reshape(values_store.shape)  14.5 us
    dot_general x2, matrix products, checkpoint_sum(): jnp.dot(train_vals[:, ckpt_index, :], test_block[ckpt_index], preferred_e...  7.51 us
    all_gather x1, waiting for transfers between devices, on_device(): gathered = lax.all_gather(test_grads, 'ex', axis=1, tiled=True)  7.15 us
    dot_general x1, matrix products, checkpoint_sum(): jnp.dot(train_vals[:, 0, :], test_block[0], preferred_element_type=jnp.fl...  3.1 us
  transfers between devices with their start and end apart: 1, of which 1 were waited for; matrix products, arithmetic and copies ran while one was open for 40% of the time, Pallas kernels for 0%

commit v1 on v0

v1 whole, which is shorter than its diff:
```python
import functools

import jax
import jax.numpy as jnp
from jax import lax
from jax.experimental import pallas as pl
from jax.experimental.pallas import tpu as pltpu
from jax.sharding import PartitionSpec as P

EPSILON = 1e-06
MESH = pl.DeviceIdType.MESH


def both(*conds):
    conds = [c for c in conds if c is not True]
    if not conds:
        return True
    out = conds[0]
    for c in conds[1:]:
        out = jnp.logical_and(out, c)
    return out


def run_if(cond, fn):
    if cond is True:
        fn()
    else:
        pl.when(cond)(fn)


def kernel(n, lines, cols, tg_ref, exps_ref, vals_hbm, lr_ref, ew_ref, w_out, sums_out,
           vals, gat, acc, ftin, ft, ftb, onehot, sums,
           recv_sem, send_sem, own_sem, vals_sem, out_sem, sum_send, sum_recv):
    ckpts, shard, queries = tg_ref.shape
    _, rows, depth = vals.shape
    blocks = exps_ref.shape[1]
    pieces = recv_sem.shape[1]
    chunks = vals_sem.shape[1]
    crows = rows // chunks

    me = lax.axis_index("ex")
    core = lax.rem(me, 2)
    chip = lax.div(me, 2)
    b = lax.rem(chip, cols)
    a = lax.div(chip, cols)

    def index(a_at, b_at, c_at):
        return (a_at * cols + b_at) * 2 + c_at

    def vals_copy(c, i):
        at = pl.ds(i * crows, crows)
        return pltpu.make_async_copy(vals_hbm.at[c, at], vals.at[c, at], vals_sem.at[c, i])

    def slot(ref, j, p):
        at = pl.ds(pl.multiple_of(j * shard, shard), shard)
        return ref.at[p, at] if pieces > 1 else ref.at[:, at]

    def own_piece(p):
        return tg_ref.at[p] if pieces > 1 else tg_ref

    own_copy = pltpu.make_async_copy(
        tg_ref, gat.at[:, pl.ds(pl.multiple_of(me * shard, shard), shard)], own_sem
    )
    own_copy.start()

    barrier = pltpu.get_barrier_semaphore()

    def greet(i, carry):
        peer = lax.rem(me + i, n)
        pl.semaphore_signal(barrier, inc=1, device_id={"ex": peer}, device_id_type=MESH)
        return carry

    lax.fori_loop(1, n, greet, 0, unroll=n <= 16)
    for c in range(ckpts):
        for i in range(chunks):
            vals_copy(c, i).start()

    a_steps = [(s, sign) for s in range(lines) for sign in ((0,) if s == 0 else (-1, 1))]
    if cols == 2:
        b_steps = [(0, 0), (1, None)]
    else:
        b_steps = [(t, sign) for t in range(cols) for sign in ((0,) if t == 0 else (-1, 1))]

    def describe(s, sa, t, sb):
        valid = []
        a_at, b_at = a, b
        if s:
            a_at = a + sa * s
            valid.append(a_at >= 0 if sa < 0 else a_at < lines)
        if t:
            if sb is None:
                b_at = 1 - b
            else:
                b_at = b + sb * t
                valid.append(b_at >= 0 if sb < 0 else b_at < cols)
        sends = []
        if t == 0:
            if s == 0 or sa < 0:
                sends.append((0, a + 1 < lines, index(a + 1, b, core)))
            if s == 0 or sa > 0:
                sends.append((1, a >= 1, index(a - 1, b, core)))
            if cols == 2:
                sends.append((2, True, index(a, 1 - b, core)))
            else:
                sends.append((2, b + 1 < cols, index(a, b + 1, core)))
                sends.append((3, b >= 1, index(a, b - 1, core)))
        elif sb is not None:
            if sb < 0:
                sends.append((2, b + 1 < cols, index(a, b + 1, core)))
            else:
                sends.append((3, b >= 1, index(a, b - 1, core)))
        sends.append((4, True, index(a, b, 1 - core)))
        return both(*valid), a_at, b_at, sends

    groups = {}
    for s, sa in a_steps:
        for t, sb in b_steps:
            groups.setdefault(s + t, []).append((t == 0 and s == 0,) + describe(s, sa, t, sb))

    def copy_of(own, a_at, b_at, direction, target, p):
        j = index(a_at, b_at, core)
        return pltpu.make_async_remote_copy(
            src_ref=own_piece(p) if own else slot(gat, j, p),
            dst_ref=slot(gat, j, p),
            send_sem=send_sem.at[direction, a_at * cols + b_at, p],
            recv_sem=recv_sem.at[j, p],
            device_id={"ex": target},
            device_id_type=MESH,
        )

    def arrived(j, p):
        return pltpu.make_async_copy(slot(gat, j, p), slot(gat, j, p), recv_sem.at[j, p])

    def forward(event, p):
        own, valid, a_at, b_at, sends = event

        def go():
            if not own:
                arrived(index(a_at, b_at, core), p).wait()
            for direction, cond, target in sends:
                run_if(cond, lambda d=direction, t=target: copy_of(own, a_at, b_at, d, t, p).start())

        run_if(valid, go)

    def settle(event, p):
        own, valid, a_at, b_at, sends = event

        def go():
            for direction, cond, target in sends:
                run_if(cond, lambda d=direction, t=target: copy_of(own, a_at, b_at, d, t, p).wait_send())

        run_if(valid, go)

    def partner_wait(event):
        _, valid, a_at, b_at, _ = event

        def go():
            for p in range(pieces):
                arrived(index(a_at, b_at, 1 - core), p).wait()

        run_if(valid, go)

    mrows = rows // 2 if rows % 32 == 0 else rows

    def product(k0, width):
        kat = pl.ds(k0, width)

        @pl.loop(0, rows // mrows)
        def _(i):
            at = pl.ds(pl.multiple_of(i * mrows, mrows), mrows)
            total = acc[at, :]
            for c in range(ckpts):
                total += lr_ref[c] * jnp.dot(
                    vals[c, at, kat], gat[c, kat, :], preferred_element_type=jnp.float32
                )
            acc[at, :] = total

    eager = (2 * shard) % 128 == 0

    def multiply(event):
        own, valid, a_at, b_at, _ = event

        def go():
            if own:
                own_copy.wait()
            partner_wait((own, True, a_at, b_at, None))
            k0 = (a_at * cols + b_at) * (2 * shard)
            product(pl.multiple_of(k0, 2 * shard), 2 * shard)

        run_if(valid, go)

    def dequantize(c, i):
        vals_copy(c, i).wait()
        sub = 48 if crows % 48 == 0 else 16

        @pl.loop(0, crows // sub)
        def _(k):
            at = pl.ds(pl.multiple_of(i * crows + k * sub, 16), sub)
            factor = jnp.dot(ftb[at, :], onehot[c], preferred_element_type=jnp.float32)
            vals[c, at, :] = vals[c, at, :] * factor.astype(jnp.bfloat16)

    pl.semaphore_wait(barrier, n - 1)
    for p in range(pieces):
        forward(groups[0][0], p)

    ftin[...] = jnp.zeros_like(ftin)
    for c in range(ckpts):
        power = jnp.left_shift(1, exps_ref[c] + 2).astype(jnp.float32) * 0.25
        ftin[c * blocks : (c + 1) * blocks, :rows] = power
    ew_at = ckpts * blocks
    ftin[ew_at : ew_at + 1, :rows] = ew_ref[...]
    for i in range(ftin.shape[1] // 128):
        turned = ftin[:, i * 128 : (i + 1) * 128].T
        ft[i * 128 : (i + 1) * 128, :] = turned
        ftb[i * 128 : (i + 1) * 128, :] = turned.astype(jnp.bfloat16)
    for c in range(ckpts):
        row = lax.broadcasted_iota(jnp.int32, onehot.shape[1:], 0)
        col = lax.broadcasted_iota(jnp.int32, onehot.shape[1:], 1)
        block = depth // blocks
        hit = (col >= (row - c * blocks) * block) & (col < (row - c * blocks + 1) * block)
        hit = hit & (row >= c * blocks) & (row < (c + 1) * blocks)
        onehot[c] = jnp.where(hit, 1.0, 0.0).astype(jnp.bfloat16)
    acc[...] = jnp.zeros_like(acc)

    units = [functools.partial(dequantize, c, i) for c in range(ckpts) for i in range(chunks)]
    for _ in range(chunks // 2):
        units.pop(0)()
    last = max(groups)
    for g in range(1, last + 1):
        for p in range(pieces):
            for event in groups[g]:
                forward(event, p)
            if g == 1:
                for _ in range(min(len(units), chunks)):
                    units.pop(0)()
        if g == 1:
            while units:
                units.pop(0)()
        if eager and g < last:
            for event in groups[g - 1]:
                multiply(event)
            if g == last - 1:
                for event in groups[g]:
                    multiply(event)
    if eager:
        for event in groups[last]:
            multiply(event)
    else:
        own_copy.wait()
        for g in range(last + 1):
            for event in groups[g]:
                partner_wait(event)
        width = 256 if depth % 256 == 0 else depth

        @pl.loop(0, depth // width)
        def _(i):
            product(pl.multiple_of(i * width, width), width)

    wrows = 48 if rows % 48 == 0 else 8

    def weigh(i, squares):
        at = pl.ds(pl.multiple_of(i * wrows, wrows), wrows)
        value = acc[at, :] * ft[at, ew_at : ew_at + 1]
        acc[at, :] = value
        return squares + jnp.sum((value * value).reshape(wrows // 8, 8, queries), axis=0)

    sums[me] = lax.fori_loop(0, rows // wrows, weigh, jnp.zeros((8, queries), jnp.float32))

    def sum_copy(peer):
        return pltpu.make_async_remote_copy(
            src_ref=sums.at[me], dst_ref=sums.at[me], send_sem=sum_send.at[peer],
            recv_sem=sum_recv.at[me], device_id={"ex": peer}, device_id_type=MESH,
        )

    def push(i, carry):
        sum_copy(lax.rem(me + i, n)).start()
        return carry

    def take(i, carry):
        source = lax.rem(me + i, n)
        pltpu.make_async_copy(sums.at[source], sums.at[source], sum_recv.at[source]).wait()
        return carry

    def sent(i, carry):
        sum_copy(lax.rem(me + i, n)).wait_send()
        return carry

    lax.fori_loop(1, n, push, 0, unroll=n <= 16)
    out_copy = pltpu.make_async_copy(acc, w_out, out_sem)
    out_copy.start()
    for g in range(last + 1):
        for event in groups[g]:
            for p in range(pieces):
                settle(event, p)
    lax.fori_loop(1, n, sent, 0, unroll=n <= 16)
    lax.fori_loop(1, n, take, 0, unroll=n <= 16)
    total = jnp.sum(sums[...], axis=0)
    sums_out[...] = jnp.sum(total, axis=0, keepdims=True)
    out_copy.wait()


def on_device(n, values_store, scale_exps, test_grads, lr_weights, example_weights):
    rows, ckpts, depth = values_store.shape
    blocks = scale_exps.shape[2]
    _, shard, queries = test_grads.shape
    chips = n // 2
    cols = 1
    while (2 * cols) ** 2 <= chips:
        cols *= 2
    lines = chips // cols
    pieces = ckpts if n <= 32 else 1
    chunks = 4 if rows % 64 == 0 else 1
    padded = -(-rows // 128) * 128
    vmem = pl.BlockSpec(memory_space=pltpu.VMEM)
    hbm = pl.BlockSpec(memory_space=pl.ANY)
    weighted, square_sums = pl.pallas_call(
        functools.partial(kernel, n, lines, cols),
        out_shape=(
            jax.ShapeDtypeStruct((rows, queries), jnp.float32),
            jax.ShapeDtypeStruct((1, queries), jnp.float32),
        ),
        in_specs=[hbm, vmem, hbm, pl.BlockSpec(memory_space=pltpu.SMEM), vmem],
        out_specs=(hbm, vmem),
        scratch_shapes=[
            pltpu.VMEM((ckpts, rows, depth), jnp.bfloat16),
            pltpu.VMEM((ckpts, n * shard, queries), jnp.bfloat16),
            pltpu.VMEM((rows, queries), jnp.float32),
            pltpu.VMEM((128, padded), jnp.float32),
            pltpu.VMEM((padded, 128), jnp.float32),
            pltpu.VMEM((padded, 128), jnp.bfloat16),
            pltpu.VMEM((ckpts, 128, depth), jnp.bfloat16),
            pltpu.VMEM((n, 8, queries), jnp.float32),
            pltpu.SemaphoreType.DMA((n, pieces)),
            pltpu.SemaphoreType.DMA((5, chips, pieces)),
            pltpu.SemaphoreType.DMA,
            pltpu.SemaphoreType.DMA((ckpts, chunks)),
            pltpu.SemaphoreType.DMA,
            pltpu.SemaphoreType.DMA((n,)),
            pltpu.SemaphoreType.DMA((n,)),
        ],
        compiler_params=pltpu.CompilerParams(
            collective_id=0, has_side_effects=True, vmem_limit_bytes=48 * 1024 * 1024
        ),
    )(
        test_grads,
        jnp.transpose(scale_exps, (1, 2, 0)),
        jnp.transpose(values_store, (1, 0, 2)),
        lr_weights,
        example_weights[None, :],
    )
    return weighted / jnp.sqrt(square_sums / (rows * n) + EPSILON)


def solution(mesh):
    return jax.shard_map(
        functools.partial(on_device, mesh.shape["ex"]),
        mesh=mesh,
        in_specs=(P("ex", None, None), P("ex", None, None), P(None, "ex", "grp"), P(), P("ex")),
        out_specs=P("ex", "grp"),
        check_vma=False,
    )
```

time: 110 us -> 44.7 us (0.41)
  Pallas kernels: 0 us -> 40.3 us
  blocking collectives: 31.5 us -> 0 us
  local copies, waits for them, and re-layouts: 29 us -> 3.19 us
  other arithmetic: 16.5 us -> 1.03 us
  between operations: 13.4 us -> 0.02 us
  matrix products: 10.6 us -> 0 us
  waiting for transfers between devices: 7.86 us -> 0 us
    pallas_call x0 -> x1, Pallas kernels: none -> 40.3 us  [on_device(): pl.pallas_call(functools.partial(kernel, n, lines, cols), out_shape=(jax....]
    psum x1 -> x0, blocking collectives: 31.5 us -> none  [on_device(): square_sums = lax.psum(jnp.sum(weighted * weighted, axis=0), 'ex')]
    mul x2 -> x0, local copies, waits for them, and re-layouts: 26.6 us -> none  [dequantize(): return (shaped * factor[..., None]).reshape(values_store.shape)]
    mul x1 -> x0, other arithmetic: 14.5 us -> none  [dequantize(): return (shaped * factor[..., None]).reshape(values_store.shape)]
    dot_general x3 -> x0, matrix products: 10.6 us -> none  [the longest x2 7.51 us: checkpoint_sum(): jnp.dot(train_vals[:, ckpt_index, :], test_block[ckpt_index], preferred_e...]
    all_gather x1 -> x0, waiting for transfers between devices: 7.15 us -> none  [on_device(): gathered = lax.all_gather(test_grads, 'ex', axis=1, tiled=True)]
    unnamed x6 -> x8, local copies, waits for them, and re-layouts: 1.4 us -> 3.19 us
  transfers between devices with their start and end apart: 1 -> 0, of which waited for: 1 -> 0; matrix products, arithmetic and copies ran while one was open for 40% -> 0% of each run, Pallas kernels for 0% -> 0%
where the time goes in v1:
time: 44.7 us; the launch traced here: 44.5 us
  Pallas kernels  40.3 us (90%)
  local copies, waits for them, and re-layouts  3.19 us (7%)
  other arithmetic  1.03 us (2%)
    pallas_call x1, Pallas kernels, on_device(): pl.pallas_call(functools.partial(kernel, n, lines, cols), out_shape=(jax....  40.3 us
    unnamed x8, local copies, waits for them, and re-layouts  3.19 us
    div x1, other arithmetic, on_device(): return weighted / jnp.sqrt(square_sums / (rows * n) + EPSILON)  1.02 us

profile of v1, /device:TPU:0, one launch (start us, length us, event | category | flops | bytes accessed | tf_op | source)
XLA Modules:
  0.0 44.5 jit_solution(3173309372159624651)
XLA Ops:
  0.0 0.0 copy-start
  0.0 0.9 %copy-done = bf16[3,128,256]{2,1,0:T(8,128)(2,1)S(1)} copy-done((bf16[3,128,256]{2,1,0:T(8,128)(2,1)S(1)}, bf16[3,128,256]{2,1,0:T(8,128)(2,1)}, u32[]{:S(2)}) %copy-start) | copy-done | bytes 196632
  0.9 0.0 copy-start.1
  0.9 0.9 %copy-done.1 = s32[960,3,16]{0,2,1:T(8,128)S(1)} copy-done((s32[960,3,16]{0,2,1:T(8,128)S(1)}, s32[960,3,16]{0,2,1:T(8,128)}, u32[]{:S(2)}) %copy-start.1) | copy-done | bytes 184344
  1.9 0.0 copy-start.2
  1.9 0.7 %copy-done.2 = f32[960]{0:T(1024)S(1)} copy-done((f32[960]{0:T(1024)S(1)}, f32[960]{0:T(1024)}, u32[]{:S(2)}) %copy-start.2) | copy-done | bytes 3864
  2.5 0.0 copy-start.3
  2.5 0.7 %copy-done.3 = f32[3]{0:T(128)S(1)} copy-done((f32[3]{0:T(128)S(1)}, f32[3]{0:T(128)}, u32[]{:S(2)}) %copy-start.3) | copy-done | bytes 36
  3.2 40.3 %shard_map.55 = (f32[960,256]{1,0:T(8,128)S(1)}, f32[1,256]{1,0:T(1,128)S(1)}) custom-call(bf16[3,128,256]{2,1,0:T(8,128)(2,1)S(1)} %copy-done, s32[3,16,960]{2,1,0:T(8,128)S(1)} %bitcast.4, bf16[3,960,2048]{2,1,0:T(8,128)(2,1)} %bitcast.6, f32[3]{0:T(128)S(1)} %copy-done.3, f32[1,960]{1,0:T(1,128)S(1)} %bitcast.5), custom_call_target="tpu_custom_call" | custom-call | tf_op jit(solution)/shard_map/pallas_call | solution.py:316
  43.5 1.0 %broadcast_divide_fusion = f32[960,256]{1,0:T(8,128)} fusion(f32[960,256]{1,0:T(8,128)S(1)} %get-tuple-element.7, f32[256]{0:T(256)S(1)} %bitcast.7), kind=kLoop, calls=%fused_computation | loop fusion | flops 245760 | bytes 1967104 | tf_op jit(solution)/shard_map/div | solution.py:351
  (1 shorter events, 0.0 us)
Async XLA Ops:
  0.0 0.9 %copy-start = (bf16[3,128,256]{2,1,0:T(8,128)(2,1)S(1)}, bf16[3,128,256]{2,1,0:T(8,128)(2,1)}, u32[]{:S(2)}) copy-start(bf16[3,128,256]{2,1,0:T(8,128)(2,1)} %tg_ref.1) | copy-start | bytes 589828
  0.9 0.9 %copy-start.1 = (s32[960,3,16]{0,2,1:T(8,128)S(1)}, s32[960,3,16]{0,2,1:T(8,128)}, u32[]{:S(2)}) copy-start(s32[960,3,16]{0,2,1:T(8,128)} %param.6) | copy-start | bytes 552964
  1.9 0.7 %copy-start.2 = (f32[960]{0:T(1024)S(1)}, f32[960]{0:T(1024)}, u32[]{:S(2)}) copy-start(f32[960]{0:T(1024)} %param.9) | copy-start | bytes 11524
  2.5 0.7 %copy-start.3 = (f32[3]{0:T(128)S(1)}, f32[3]{0:T(128)}, u32[]{:S(2)}) copy-start(f32[3]{0:T(128)} %lr_ref.1) | copy-start | bytes 40

commit v2 on v1

--- a/solution.py
+++ b/solution.py
@@ -24,16 +24,18 @@
 def run_if(cond, fn):
     if cond is True:
         fn()
-    else:
+    elif cond is not False:
         pl.when(cond)(fn)
 
 
-def kernel(n, lines, cols, tg_ref, exps_ref, vals_hbm, lr_ref, ew_ref, w_out, sums_out,
-           vals, gat, acc, ftin, ft, ftb, onehot, sums,
+def kernel(n, lines, cols, tg_ref, exps_hbm, vals_hbm, lr_hbm, ew_hbm, w_out, sums_out,
+           exps_ref, lr_ref, ew_ref, small_sem, vals, gat, acc, ftin, ft, sums,
            recv_sem, send_sem, own_sem, vals_sem, out_sem, sum_send, sum_recv):
     ckpts, shard, queries = tg_ref.shape
-    _, rows, depth = vals.shape
+    _, parts, rows, width = vals.shape
     blocks = exps_ref.shape[1]
+    depth = parts * width
+    block = depth // blocks
     pieces = recv_sem.shape[1]
     chunks = vals_sem.shape[1]
     crows = rows // chunks
@@ -49,7 +51,12 @@
 
     def vals_copy(c, i):
         at = pl.ds(i * crows, crows)
-        return pltpu.make_async_copy(vals_hbm.at[c, at], vals.at[c, at], vals_sem.at[c, i])
+        return [
+            pltpu.make_async_copy(
+                vals_hbm.at[c, at, k * width : (k + 1) * width], vals.at[c, k, at], vals_sem.at[c, i, k]
+            )
+            for k in range(parts)
+        ]
 
     def slot(ref, j, p):
         at = pl.ds(pl.multiple_of(j * shard, shard), shard)
@@ -61,7 +68,11 @@
     own_copy = pltpu.make_async_copy(
         tg_ref, gat.at[:, pl.ds(pl.multiple_of(me * shard, shard), shard)], own_sem
     )
-    own_copy.start()
+    small = [
+        pltpu.make_async_copy(exps_hbm, exps_ref, small_sem.at[0]),
+        pltpu.make_async_copy(ew_hbm, ew_ref, small_sem.at[1]),
+        pltpu.make_async_copy(lr_hbm, lr_ref, small_sem.at[2]),
+    ]
 
     barrier = pltpu.get_barrier_semaphore()
 
@@ -71,9 +82,13 @@
         return carry
 
     lax.fori_loop(1, n, greet, 0, unroll=n <= 16)
+    for copy in small:
+        copy.start()
+    own_copy.start()
     for c in range(ckpts):
         for i in range(chunks):
-            vals_copy(c, i).start()
+            for copy in vals_copy(c, i):
+                copy.start()
 
     a_steps = [(s, sign) for s in range(lines) for sign in ((0,) if s == 0 else (-1, 1))]
     if cols == 2:
@@ -100,11 +115,16 @@
             if s == 0 or sa > 0:
                 sends.append((1, a >= 1, index(a - 1, b, core)))
             if cols == 2:
-                sends.append((2, True, index(a, 1 - b, core)))
+                sends.append((2, True if s == 0 else "rows first", index(a, 1 - b, core)))
             else:
                 sends.append((2, b + 1 < cols, index(a, b + 1, core)))
                 sends.append((3, b >= 1, index(a, b - 1, core)))
-        elif sb is not None:
+        elif sb is None:
+            if s == 0 or sa < 0:
+                sends.append((0, ("columns first", a + 1 < lines), index(a + 1, b, core)))
+            if s == 0 or sa > 0:
+                sends.append((1, ("columns first", a >= 1), index(a - 1, b, core)))
+        else:
             if sb < 0:
                 sends.append((2, b + 1 < cols, index(a, b + 1, core)))
             else:
@@ -128,6 +148,13 @@
             device_id_type=MESH,
         )
 
+    def choose(cond, p):
+        if cond == "rows first":
+            return core == 1 if p == pieces - 1 else True
+        if isinstance(cond, tuple):
+            return jnp.logical_and(cond[1], core == 0) if p == pieces - 1 else False
+        return cond
+
     def arrived(j, p):
         return pltpu.make_async_copy(slot(gat, j, p), slot(gat, j, p), recv_sem.at[j, p])
 
@@ -138,7 +165,7 @@
             if not own:
                 arrived(index(a_at, b_at, core), p).wait()
             for direction, cond, target in sends:
-                run_if(cond, lambda d=direction, t=target: copy_of(own, a_at, b_at, d, t, p).start())
+                run_if(choose(cond, p), lambda d=direction, t=target: copy_of(own, a_at, b_at, d, t, p).start())
 
         run_if(valid, go)
 
@@ -147,7 +174,7 @@
 
         def go():
             for direction, cond, target in sends:
-                run_if(cond, lambda d=direction, t=target: copy_of(own, a_at, b_at, d, t, p).wait_send())
+                run_if(choose(cond, p), lambda d=direction, t=target: copy_of(own, a_at, b_at, d, t, p).wait_send())
 
         run_if(valid, go)
 
@@ -162,8 +189,8 @@
 
     mrows = rows // 2 if rows % 32 == 0 else rows
 
-    def product(k0, width):
-        kat = pl.ds(k0, width)
+    def product(part):
+        kat = pl.ds(pl.multiple_of(part * width, width), width)
 
         @pl.loop(0, rows // mrows)
         def _(i):
@@ -171,11 +198,11 @@
             total = acc[at, :]
             for c in range(ckpts):
                 total += lr_ref[c] * jnp.dot(
-                    vals[c, at, kat], gat[c, kat, :], preferred_element_type=jnp.float32
+                    vals[c, part, at, :], gat[c, kat, :], preferred_element_type=jnp.float32
                 )
             acc[at, :] = total
 
-    eager = (2 * shard) % 128 == 0
+    eager = 2 * shard == width
 
     def multiply(event):
         own, valid, a_at, b_at, _ = event
@@ -184,25 +211,26 @@
             if own:
                 own_copy.wait()
             partner_wait((own, True, a_at, b_at, None))
-            k0 = (a_at * cols + b_at) * (2 * shard)
-            product(pl.multiple_of(k0, 2 * shard), 2 * shard)
+            product(a_at * cols + b_at)
 
         run_if(valid, go)
 
     def dequantize(c, i):
-        vals_copy(c, i).wait()
-        sub = 48 if crows % 48 == 0 else 16
-
-        @pl.loop(0, crows // sub)
-        def _(k):
-            at = pl.ds(pl.multiple_of(i * crows + k * sub, 16), sub)
-            factor = jnp.dot(ftb[at, :], onehot[c], preferred_element_type=jnp.float32)
-            vals[c, at, :] = vals[c, at, :] * factor.astype(jnp.bfloat16)
+        for copy in vals_copy(c, i):
+            copy.wait()
+        at = pl.ds(i * crows, crows)
+        for j in range(blocks):
+            part, lane = divmod(j * block, width)
+            factor = jnp.broadcast_to(ft[at, c * blocks + j : c * blocks + j + 1], (crows, block))
+            kat = slice(lane, lane + block)
+            vals[c, part, at, kat] = vals[c, part, at, kat] * factor.astype(jnp.bfloat16)
 
     pl.semaphore_wait(barrier, n - 1)
     for p in range(pieces):
         forward(groups[0][0], p)
 
+    for copy in small:
+        copy.wait()
     ftin[...] = jnp.zeros_like(ftin)
     for c in range(ckpts):
         power = jnp.left_shift(1, exps_ref[c] + 2).astype(jnp.float32) * 0.25
@@ -210,16 +238,7 @@
     ew_at = ckpts * blocks
     ftin[ew_at : ew_at + 1, :rows] = ew_ref[...]
     for i in range(ftin.shape[1] // 128):
-        turned = ftin[:, i * 128 : (i + 1) * 128].T
-        ft[i * 128 : (i + 1) * 128, :] = turned
-        ftb[i * 128 : (i + 1) * 128, :] = turned.astype(jnp.bfloat16)
-    for c in range(ckpts):
-        row = lax.broadcasted_iota(jnp.int32, onehot.shape[1:], 0)
-        col = lax.broadcasted_iota(jnp.int32, onehot.shape[1:], 1)
-        block = depth // blocks
-        hit = (col >= (row - c * blocks) * block) & (col < (row - c * blocks + 1) * block)
-        hit = hit & (row >= c * blocks) & (row < (c + 1) * blocks)
-        onehot[c] = jnp.where(hit, 1.0, 0.0).astype(jnp.bfloat16)
+        ft[i * 128 : (i + 1) * 128, :] = ftin[:, i * 128 : (i + 1) * 128].T
     acc[...] = jnp.zeros_like(acc)
 
     units = [functools.partial(dequantize, c, i) for c in range(ckpts) for i in range(chunks)]
@@ -250,21 +269,18 @@
         for g in range(last + 1):
             for event in groups[g]:
                 partner_wait(event)
-        width = 256 if depth % 256 == 0 else depth
-
-        @pl.loop(0, depth // width)
-        def _(i):
-            product(pl.multiple_of(i * width, width), width)
-
-    wrows = 48 if rows % 48 == 0 else 8
-
-    def weigh(i, squares):
-        at = pl.ds(pl.multiple_of(i * wrows, wrows), wrows)
+        pl.loop(0, parts)(product)
+
+    squares = jnp.zeros((8, queries), jnp.float32)
+    outs = []
+    for i in range(chunks):
+        at = slice(i * crows, (i + 1) * crows)
         value = acc[at, :] * ft[at, ew_at : ew_at + 1]
         acc[at, :] = value
-        return squares + jnp.sum((value * value).reshape(wrows // 8, 8, queries), axis=0)
-
-    sums[me] = lax.fori_loop(0, rows // wrows, weigh, jnp.zeros((8, queries), jnp.float32))
+        outs.append(pltpu.make_async_copy(acc.at[at], w_out.at[at], out_sem.at[i]))
+        outs[-1].start()
+        squares += jnp.sum((value * value).reshape(crows // 8, 8, queries), axis=0)
+    sums[me] = jnp.sum(squares, axis=0, keepdims=True)
 
     def sum_copy(peer):
         return pltpu.make_async_remote_copy(
@@ -286,17 +302,15 @@
         return carry
 
     lax.fori_loop(1, n, push, 0, unroll=n <= 16)
-    out_copy = pltpu.make_async_copy(acc, w_out, out_sem)
-    out_copy.start()
     for g in range(last + 1):
         for event in groups[g]:
             for p in range(pieces):
                 settle(event, p)
     lax.fori_loop(1, n, sent, 0, unroll=n <= 16)
     lax.fori_loop(1, n, take, 0, unroll=n <= 16)
-    total = jnp.sum(sums[...], axis=0)
-    sums_out[...] = jnp.sum(total, axis=0, keepdims=True)
-    out_copy.wait()
+    sums_out[...] = jnp.sum(sums[...], axis=0)
+    for copy in outs:
+        copy.wait()
 
 
 def on_device(n, values_store, scale_exps, test_grads, lr_weights, example_weights):
@@ -310,36 +324,39 @@
     lines = chips // cols
     pieces = ckpts if n <= 32 else 1
     chunks = 4 if rows % 64 == 0 else 1
+    parts = depth // 256 if depth % 256 == 0 else 1
     padded = -(-rows // 128) * 128
     vmem = pl.BlockSpec(memory_space=pltpu.VMEM)
-    hbm = pl.BlockSpec(memory_space=pl.ANY)
+    hbm = pl.BlockSpec(memory_space=pltpu.HBM)
     weighted, square_sums = pl.pallas_call(
         functools.partial(kernel, n, lines, cols),
         out_shape=(
             jax.ShapeDtypeStruct((rows, queries), jnp.float32),
             jax.ShapeDtypeStruct((1, queries), jnp.float32),
         ),
-        in_specs=[hbm, vmem, hbm, pl.BlockSpec(memory_space=pltpu.SMEM), vmem],
-        out_specs=(hbm, vmem),
+        in_specs=[hbm] * 5,
+        out_specs=(pl.BlockSpec(memory_space=pl.ANY), vmem),
         scratch_shapes=[
-            pltpu.VMEM((ckpts, rows, depth), jnp.bfloat16),
+            pltpu.VMEM((ckpts, blocks, rows), jnp.int32),
+            pltpu.SMEM((ckpts,), jnp.float32),
+            pltpu.VMEM((1, rows), jnp.float32),
+            pltpu.SemaphoreType.DMA((3,)),
+            pltpu.VMEM((ckpts, parts, rows, depth // parts), jnp.bfloat16),
             pltpu.VMEM((ckpts, n * shard, queries), jnp.bfloat16),
             pltpu.VMEM((rows, queries), jnp.float32),
             pltpu.VMEM((128, padded), jnp.float32),
             pltpu.VMEM((padded, 128), jnp.float32),
-            pltpu.VMEM((padded, 128), jnp.bfloat16),
-            pltpu.VMEM((ckpts, 128, depth), jnp.bfloat16),
-            pltpu.VMEM((n, 8, queries), jnp.float32),
+            pltpu.VMEM((n, 1, queries), jnp.float32),
             pltpu.SemaphoreType.DMA((n, pieces)),
             pltpu.SemaphoreType.DMA((5, chips, pieces)),
             pltpu.SemaphoreType.DMA,
-            pltpu.SemaphoreType.DMA((ckpts, chunks)),
-            pltpu.SemaphoreType.DMA,
+            pltpu.SemaphoreType.DMA((ckpts, chunks, parts)),
+            pltpu.SemaphoreType.DMA((chunks,)),
             pltpu.SemaphoreType.DMA((n,)),
             pltpu.SemaphoreType.DMA((n,)),
         ],
         compiler_params=pltpu.CompilerParams(
-            collective_id=0, has_side_effects=True, vmem_limit_bytes=48 * 1024 * 1024
+            collective_id=0, has_side_effects=True, vmem_limit_bytes=60 * 1024 * 1024
         ),
     )(
         test_grads,

time: 44.7 us -> 38.2 us (0.85)
  Pallas kernels: 40.3 us -> 35.2 us
  local copies, waits for them, and re-layouts: 3.19 us -> 0 us
  other arithmetic: 1.03 us -> 2.9 us
    pallas_call x1, Pallas kernels: 40.3 us -> 35.2 us  [on_device(): pl.pallas_call(functools.partial(kernel, n, lines, cols), out_shape=(jax....]
    unnamed x8 -> x0, local copies, waits for them, and re-layouts: 3.19 us -> none
    div x1, other arithmetic: 1.02 us -> 2.22 us  [on_device(): return weighted / jnp.sqrt(square_sums / (rows * n) + EPSILON)]
    sqrt x1, other arithmetic: 0.01 us -> 0.68 us  [on_device(): return weighted / jnp.sqrt(square_sums / (rows * n) + EPSILON)]
where the time goes in v2:
time: 38.2 us; the launch traced here: 38.1 us
  Pallas kernels  35.2 us (92%)
  other arithmetic  2.9 us (8%)
    pallas_call x1, Pallas kernels, on_device(): pl.pallas_call(functools.partial(kernel, n, lines, cols), out_shape=(jax....  35.2 us
    div x1, other arithmetic, on_device(): return weighted / jnp.sqrt(square_sums / (rows * n) + EPSILON)  2.22 us

profile of v2, /device:TPU:0, one launch (start us, length us, event | category | flops | bytes accessed | tf_op | source)
XLA Modules:
  0.0 38.1 jit_solution(5768245845421725132)
XLA Ops:
  0.0 35.2 %shard_map.55 = (f32[960,256]{1,0:T(8,128)}, f32[1,256]{1,0:T(1,128)}) custom-call(bf16[3,128,256]{2,1,0:T(8,128)(2,1)} %tg_ref.1, s32[3,16,960]{2,1,0:T(8,128)} %bitcast.5, bf16[3,960,2048]{2,1,0:T(8,128)(2,1)} %bitcast.4, f32[3]{0:T(128)} %lr_hbm.1, f32[1,960]{1,0:T(1,128)} %bitcast.7), custom_call_target="tpu_custom_call" | custom-call | tf_op jit(solution)/shard_map/pallas_call | solution.py:331
  35.2 0.7 %add_sqrt_fusion = f32[1,256]{1,0:T(1,128)S(1)} fusion(f32[1,256]{1,0:T(1,128)} %get-tuple-element.8), kind=kLoop, calls=%fused_computation.1 | loop fusion | flops 512 | bytes 2048 | tf_op jit(solution)/shard_map/sqrt | solution.py:368
  35.8 2.2 %broadcast_divide_fusion = f32[960,256]{1,0:T(8,128)} fusion(f32[960,256]{1,0:T(8,128)} %get-tuple-element.7, f32[256]{0:T(256)S(1)} %bitcast.6), kind=kLoop, calls=%fused_computation | loop fusion | flops 245760 | bytes 1967104 | tf_op jit(solution)/shard_map/div | solution.py:368

commit v3 on v2

--- a/solution.py
+++ b/solution.py
@@ -135,7 +135,8 @@
     groups = {}
     for s, sa in a_steps:
         for t, sb in b_steps:
-            groups.setdefault(s + t, []).append((t == 0 and s == 0,) + describe(s, sa, t, sb))
+            groups.setdefault(2 * s + 3 * t, []).append((t == 0 and s == 0,) + describe(s, sa, t, sb))
+    groups = [groups[key] for key in sorted(groups)]
 
     def copy_of(own, a_at, b_at, direction, target, p):
         j = index(a_at, b_at, core)
@@ -242,25 +243,32 @@
     acc[...] = jnp.zeros_like(acc)
 
     units = [functools.partial(dequantize, c, i) for c in range(ckpts) for i in range(chunks)]
-    for _ in range(chunks // 2):
-        units.pop(0)()
-    last = max(groups)
+    last = len(groups) - 1
+    settled = 0
     for g in range(1, last + 1):
+        if g == last:
+            while settled < last - 2:
+                for event in groups[settled]:
+                    for p in range(pieces):
+                        settle(event, p)
+                settled += 1
         for p in range(pieces):
             for event in groups[g]:
                 forward(event, p)
-            if g == 1:
-                for _ in range(min(len(units), chunks)):
+            for _ in range(2):
+                if units:
                     units.pop(0)()
-        if g == 1:
+        if g >= 2:
             while units:
                 units.pop(0)()
-        if eager and g < last:
-            for event in groups[g - 1]:
+        if eager and 2 <= g < last:
+            for event in groups[g - 2]:
                 multiply(event)
             if g == last - 1:
-                for event in groups[g]:
+                for event in groups[g - 1] + groups[g]:
                     multiply(event)
+    while units:
+        units.pop(0)()
     if eager:
         for event in groups[last]:
             multiply(event)
@@ -302,7 +310,7 @@
         return carry
 
     lax.fori_loop(1, n, push, 0, unroll=n <= 16)
-    for g in range(last + 1):
+    for g in range(settled, last + 1):
         for event in groups[g]:
             for p in range(pieces):
                 settle(event, p)

time: 38.2 us -> 36.8 us (0.963)
  Pallas kernels: 35.2 us -> 33.8 us
    pallas_call x1, Pallas kernels: 35.2 us -> 33.8 us  [on_device(): pl.pallas_call(functools.partial(kernel, n, lines, cols), out_shape=(jax....]
where the time goes in v3:
time: 36.8 us; the launch traced here: 36.7 us
  Pallas kernels  33.8 us (92%)
  other arithmetic  2.9 us (8%)
    pallas_call x1, Pallas kernels, on_device(): pl.pallas_call(functools.partial(kernel, n, lines, cols), out_shape=(jax....  33.8 us
    div x1, other arithmetic, on_device(): return weighted / jnp.sqrt(square_sums / (rows * n) + EPSILON)  2.22 us

profile of v3, /device:TPU:0, one launch (start us, length us, event | category | flops | bytes accessed | tf_op | source)
XLA Modules:
  0.0 36.7 jit_solution(3401432537522454769)
XLA Ops:
  0.0 33.8 %shard_map.55 = (f32[960,256]{1,0:T(8,128)}, f32[1,256]{1,0:T(1,128)}) custom-call(bf16[3,128,256]{2,1,0:T(8,128)(2,1)} %tg_ref.1, s32[3,16,960]{2,1,0:T(8,128)} %bitcast.5, bf16[3,960,2048]{2,1,0:T(8,128)(2,1)} %bitcast.4, f32[3]{0:T(128)} %lr_hbm.1, f32[1,960]{1,0:T(1,128)} %bitcast.7), custom_call_target="tpu_custom_call" | custom-call | tf_op jit(solution)/shard_map/pallas_call | solution.py:339
  33.8 0.7 %add_sqrt_fusion = f32[1,256]{1,0:T(1,128)S(1)} fusion(f32[1,256]{1,0:T(1,128)} %get-tuple-element.8), kind=kLoop, calls=%fused_computation.1 | loop fusion | flops 512 | bytes 2048 | tf_op jit(solution)/shard_map/sqrt | solution.py:376
  34.5 2.2 %broadcast_divide_fusion = f32[960,256]{1,0:T(8,128)} fusion(f32[960,256]{1,0:T(8,128)} %get-tuple-element.7, f32[256]{0:T(256)S(1)} %bitcast.6), kind=kLoop, calls=%fused_computation | loop fusion | flops 245760 | bytes 1967104 | tf_op jit(solution)/shard_map/div | solution.py:376
